TPU v7x, 32 devices: a whole 2x2x4 slice. The times are simulated.
32 devices in a mesh: grp: 2 (over y), seq: 8 (over z, x), mdl: 2 (over core).
Axes of the slice: x: 2, y: 2, z: 4, core: 2. Of those that a mesh axis runs over, the one named last changes fastest.
Arguments:
- vis_tokens: bfloat16 [2048, 1152], P(('grp', 'seq'), 'mdl'), parts along dimension 0, may hold values from -6 to 6
- merge_target: int32 [2048], P(('grp', 'seq')), parts along dimension 0, may hold values from 0 to 126, as said below
- merged_counts: int32 [16], P('grp'), parts along dimension 0, may hold values from 43 to 127, as said below
- proj_weight: bfloat16 [1152, 3584], P('mdl'), may hold values from -0.1875 to 0.1875
- norm_gain: float32 [3584], replicated, may hold values from 0.1 to 1.9
- query_weight: bfloat16 [3584, 1792], P('seq', 'mdl'), may hold values from -0.09375 to 0.09375
- keyval_weight: bfloat16 [3584, 2, 256], P('seq', 'mdl'), may hold values from -0.09375 to 0.09375
- cache_kv: bfloat16 [512, 2, 256], P(('grp', 'seq'), 'mdl'), parts along dimension 0, may hold values from -40 to 40
Outputs:
- attn_out: bfloat16 [64, 16, 1792], P(None, ('grp', 'seq'), 'mdl'), parts along dimension 1
- new_kv: bfloat16 [64, 16, 2, 256], P(None, ('grp', 'seq'), 'mdl'), parts along dimension 1
There are 2 independent parts, one for each index of `grp`. A program takes and returns all parts, laid end to end along the dimension named above; an argument that names none is the same for every part. Nothing has to cross between parts.
Inputs may be any that keep to these rules, and one draw needn't show every extreme that they name: `merge_target`: each shard's targets lie below that shard's entry of merged_counts, and every row index below that entry is named by at least one token of the shard. `merged_counts`: the counts sum to 512.
All inputs are finite; a program needn't handle non-finite values.
Results may differ from a plain program's by a relative error of at most 0.011.
Values may be sent and summed in bfloat16 or wider, within the bound.
A program may use at most 64 MiB of HBM per device.

v0:
```python
import math

import jax
import jax.numpy as jnp
from jax import lax
from jax.sharding import PartitionSpec as P

theta_base = 1000000.0
norm_eps = 1e-06
mask_fill = -1e30


def rotate(head_rows, positions):
    half_dim = head_rows.shape[-1] // 2
    frequency = jnp.power(
        theta_base, -2.0 * jnp.arange(half_dim, dtype=jnp.float32) / head_rows.shape[-1]
    )
    angles = positions.astype(jnp.float32)[:, None] * frequency[None, :]
    cosine = jnp.concatenate([jnp.cos(angles), jnp.cos(angles)], axis=-1)[:, None, :]
    sine_part = jnp.concatenate([jnp.sin(angles), jnp.sin(angles)], axis=-1)[:, None, :]
    front_half = head_rows[..., :half_dim]
    back_half = head_rows[..., half_dim:]
    turned = jnp.concatenate([-back_half, front_half], axis=-1)
    return head_rows * cosine + turned * sine_part


def per_device(
    vis_tokens,
    merge_target,
    merged_counts,
    proj_weight,
    norm_gain,
    query_weight,
    keyval_weight,
    cache_kv,
):
    shards = lax.axis_size("seq")
    device_index = lax.axis_index("seq")
    tok_in, width_in = vis_tokens.shape
    new_dev = tok_in // 2
    slot_cap = (new_dev + 3 * (new_dev // 3) + shards - 1) // shards
    offsets = jnp.cumsum(merged_counts) - merged_counts
    count_here = merged_counts[device_index]
    offset_here = offsets[device_index]
    slot_rows = jnp.arange(tok_in, dtype=jnp.int32)
    chosen = slot_rows[:, None] == merge_target[None, :]
    sizes = jnp.sum(chosen.astype(jnp.float32), axis=1)
    summed = jnp.dot(chosen.astype(jnp.bfloat16), vis_tokens, preferred_element_type=jnp.float32)
    merged = (summed / jnp.where(sizes > 0.0, sizes, 1.0)[:, None]).astype(jnp.bfloat16)
    peer_ids = jnp.arange(shards, dtype=jnp.int32)
    slot_ids = jnp.arange(slot_cap, dtype=jnp.int32)
    local_row = jnp.mod(peer_ids - offset_here, shards)[:, None] + slot_ids[None, :] * shards
    is_valid = local_row < count_here
    picked = jnp.take(merged, jnp.minimum(local_row, tok_in - 1).reshape(-1), axis=0).reshape(
        shards, slot_cap, width_in
    )
    outgoing = jnp.where(is_valid[:, :, None], picked, jnp.zeros_like(picked))
    incoming = lax.all_to_all(outgoing, "seq", split_axis=0, concat_axis=0, tiled=True)
    first_row = offsets + jnp.mod(device_index - offsets, shards)
    global_row = first_row[:, None] + slot_ids[None, :] * shards
    arrived = global_row < (offsets + merged_counts)[:, None]
    target = jnp.where(arrived, global_row // shards, -1).reshape(-1)
    placing = jnp.arange(new_dev, dtype=jnp.int32)[:, None] == target[None, :]
    arrived_rows = jnp.dot(
        placing.astype(jnp.bfloat16),
        incoming.reshape(shards * slot_cap, width_in),
        preferred_element_type=jnp.float32,
    ).astype(jnp.bfloat16)
    partial_pre = jnp.dot(arrived_rows, proj_weight, preferred_element_type=jnp.float32)
    pre_act = lax.psum(partial_pre, "mdl")
    activated = jax.nn.gelu(pre_act, approximate=False)
    inv_rms = lax.rsqrt(jnp.mean(activated * activated, axis=1, keepdims=True) + norm_eps)
    normed = (activated * inv_rms * norm_gain[None, :]).astype(jnp.bfloat16)

    def add_rows(piece):
        return jnp.dot(
            normed, piece.reshape(piece.shape[0], -1), preferred_element_type=jnp.float32
        )

    kv_heads = keyval_weight.shape[1]
    head_dim = keyval_weight.shape[2] // 2
    q_raw = add_rows(lax.all_gather(query_weight, "seq", axis=0, tiled=True))
    kv_raw = add_rows(lax.all_gather(keyval_weight, "seq", axis=0, tiled=True))
    cache_rows = cache_kv.shape[0]
    query_global = jnp.arange(new_dev, dtype=jnp.int32) * shards + device_index
    positions = cache_rows * shards + query_global
    heads_here = query_weight.shape[1] // head_dim
    group = heads_here // kv_heads
    queries = rotate(q_raw.reshape(new_dev, heads_here, head_dim), positions).astype(jnp.bfloat16)
    kv_rows = kv_raw.reshape(new_dev, kv_heads, 2 * head_dim)
    fresh = jnp.concatenate(
        [rotate(kv_rows[..., :head_dim], positions), kv_rows[..., head_dim:]], axis=-1
    ).astype(jnp.bfloat16)
    query_rows = (
        queries.reshape(new_dev, kv_heads, group, head_dim)
        .transpose(1, 0, 2, 3)
        .reshape(kv_heads, new_dev * group, head_dim)
    )
    query_pos = jnp.repeat(query_global, group)
    context = jnp.concatenate([cache_kv, fresh], axis=0)
    stride = cache_rows + new_dev
    inv_scale = 1.0 / math.sqrt(head_dim)

    def absorb(carried, key_block, visible):
        row_max, totals, accumulated = carried
        scores = (
            jnp.einsum(
                "hqd,khd->hqk",
                query_rows,
                key_block[:, :, :head_dim],
                preferred_element_type=jnp.float32,
            )
            * inv_scale
        )
        scores = jnp.where(visible[None], scores, mask_fill)
        new_max = jnp.maximum(row_max, jnp.max(scores, axis=2))
        weights = jnp.where(visible[None], jnp.exp(scores - new_max[:, :, None]), 0.0)
        factor = jnp.exp(row_max - new_max)
        totals = totals * factor + jnp.sum(weights, axis=2)
        mixed = jnp.einsum(
            "hqk,khd->hqd",
            weights.astype(jnp.bfloat16),
            key_block[:, :, head_dim:],
            preferred_element_type=jnp.float32,
        )
        accumulated = accumulated * factor[:, :, None] + mixed
        return (new_max, totals, accumulated)

    lanes = new_dev * group
    start_state = (
        jnp.full((kv_heads, lanes), mask_fill, jnp.float32),
        jnp.zeros((kv_heads, lanes), jnp.float32),
        jnp.zeros((kv_heads, lanes, head_dim), jnp.float32),
    )
    piece = lax.all_gather(context, "seq", axis=0, tiled=True)
    rows_in = piece.shape[0]
    padded_len = -(-rows_in // 128) * 128
    padded = piece
    tiles = padded_len // 128
    block_tiles = max((divisor for divisor in range(1, min(tiles, 8) + 1) if tiles % divisor == 0))
    block_len = 128 * block_tiles

    def fold_block(block_no, state_now):
        key_block = lax.dynamic_slice_in_dim(padded, block_no * block_len, block_len, 0)
        key_offset = block_no * block_len + jnp.arange(block_len, dtype=jnp.int32)
        source = key_offset // stride
        local_key = key_offset % stride
        key_global = (local_key - cache_rows) * shards + source
        present = (key_offset < rows_in)[None, :]
        visible = present & (
            (local_key < cache_rows)[None, :] | (key_global[None, :] <= query_pos[:, None])
        )
        return absorb(state_now, key_block, visible)

    row_max, totals, accumulated = lax.fori_loop(
        0, padded_len // block_len, fold_block, start_state
    )
    attended = (
        (accumulated / totals[:, :, None])
        .reshape(kv_heads, new_dev, group, head_dim)
        .transpose(1, 0, 2, 3)
    )
    attended = attended.reshape(new_dev, 1, heads_here * head_dim).astype(jnp.bfloat16)
    return (attended, fresh.reshape(new_dev, 1, kv_heads, 2 * head_dim))


def solution(mesh):
    placed = (
        P(("grp", "seq"), "mdl"),
        P(("grp", "seq")),
        P("grp"),
        P("mdl", None),
        P(),
        P("seq", "mdl"),
        P("seq", "mdl", None),
        P(("grp", "seq"), "mdl", None),
    )
    return jax.shard_map(
        per_device,
        mesh=mesh,
        in_specs=placed,
        out_specs=(P(None, ("grp", "seq"), "mdl"), P(None, ("grp", "seq"), "mdl", None)),
        check_vma=False,
    )
```

profile of v0, /device:TPU:0, one launch (start us, length us, event | category | flops | bytes accessed | tf_op | source)
XLA Modules:
  0.0 201.2 jit_solution(10335765125091353895)
XLA Ops:
  8.0 0.9 reduce-window.8
  8.9 0.7 fusion.43
  9.6 1.2 dynamic_slice.9
  11.4 0.7 and_select_fusion
  12.0 0.7 add_compare_fusion
  12.9 0.8 convert_reduce_fusion
  13.7 0.9 fusion.4
  14.8 0.9 gather_fusion
  15.6 0.8 select_select_fusion
  16.4 7.2 %all-to-all-start = ((bf16[8,16,576]{2,1,0:T(8,128)(2,1)}), bf16[8,16,576]{2,1,0:T(8,128)(2,1)S(1)}, u32[]{:S(2)}, u32[]{:S(2)}) async-start(bf16[8,16,576]{2,1,0:T(8,128)(2,1)} %select_select_fusion), calls=%async_computation | async-start | bytes 327680 | tf_op jit(solution)/shard_map/all_to_all | solution.py:58
  24.0 7.3 %all-to-all-done = bf16[8,16,576]{2,1,0:T(8,128)(2,1)S(1)} async-done(((bf16[8,16,576]{2,1,0:T(8,128)(2,1)}), bf16[8,16,576]{2,1,0:T(8,128)(2,1)S(1)}, u32[]{:S(2)}, u32[]{:S(2)}) %all-to-all-start) | async-done | bytes 147488 | tf_op jit(solution)/shard_map/all_to_all | solution.py:58
  31.2 4.1 %fusion.6 = f32[64,3584]{1,0:T(8,128)} fusion(bf16[576,3584]{1,0:T(8,128)(2,1)} %param.11, bf16[128,576]{1,0:T(8,128)(2,1)S(1)} %bitcast.51, s32[128]{0:T(128)S(1)} %compare_select_fusion.7), kind=kOutput, calls=%fused_computation.14 | convolution fusion | flops 273723392 | bytes 5194240 | tf_op jit(solution)/shard_map/dot_general | solution.py:69
  37.2 16.0 %all-reduce.2.cloned.1.call-done = f32[64,3584]{1,0:T(8,128)} async-done(((f32[64,3584]{1,0:T(8,128)}), f32[64,3584]{1,0:T(8,128)}) %all-reduce.2.cloned.1.call-update) | async-done | bytes 917520 | tf_op jit(solution)/shard_map/psum | solution.py:70
  53.2 3.3 %multiply_reduce_fusion = (f32[64]{0:T(128)S(1)}, f32[64,3584]{1,0:T(8,128)S(1)}) fusion(f32[64,3584]{1,0:T(8,128)} %all-reduce.2.cloned.1.call-done), kind=kLoop, calls=%fused_computation.19 | loop fusion | flops 15138752 | bytes 1835264 | tf_op jit(solution)/shard_map/reduce_sum | solution.py:72
  56.5 26.4 %all-gather.5.cloned.1.call-done = bf16[3584,1,256]{2,0,1:T(8,128)(2,1)} async-done(((bf16[448,1,256]{2,0,1:T(8,128)(2,1)}), bf16[3584,1,256]{2,0,1:T(8,128)(2,1)}) %all-gather.5.cloned.1.call-update) | async-done | bytes 1835024 | tf_op jit(solution)/shard_map/all_gather | solution.py:83
  82.9 2.0 fusion.7
  85.1 0.6 pad_maximum_fusion.3
  85.8 32.5 %all_gather.11 = bf16[768,1,256]{2,0,1:T(8,128)(2,1)S(1)} all-gather(bf16[96,1,256]{2,0,1:T(8,128)(2,1)S(1)} %maximum_maximum_fusion), channel_id=1, replica_groups=mesh['grp'=2,'seq'=8,'mdl'=2] {'seq'}, dimensions={0}, use_global_device_ids=true | all-gather | bytes 442368 | tf_op jit(solution)/shard_map/all_gather | solution.py:135
  118.2 68.1 %all-gather.3.cloned.1.call-done = bf16[3584,896]{1,0:T(8,128)(2,1)} async-done(((bf16[448,896]{1,0:T(8,128)(2,1)}), bf16[3584,896]{1,0:T(8,128)(2,1)}) %all-gather.3.cloned.1.call-update) | async-done | bytes 6422544 | tf_op jit(solution)/shard_map/all_gather | solution.py:82
  186.3 4.1 %fusion.49 = f32[64,896]{1,0:T(8,128)S(1)} fusion(bf16[3584,896]{1,0:T(8,128)(2,1)} %all-gather.3.cloned.1.call-done, f32[64,3584]{1,0:T(8,128)S(1)} %get-tuple-element.19, f32[3584]{0:T(1024)S(1)} %copy-done.1, f32[64]{0:T(128)S(1)} %add_rsqrt_fusion), kind=kOutput, calls=%fused_computation.116 | convolution fusion | flops 411729920 | bytes 7584000 | tf_op jit(solution)/shard_map/dot_general | solution.py:76
  191.1 0.6 fusion.51
  191.7 0.6 fusion.19
  192.4 0.6 fusion.5
  193.0 0.8 convert_element_type.74
  (51 shorter events, 3.9 us)
Async XLA Ops:
  8.0 5.7 %copy-start = (bf16[128,576]{0,1:T(8,128)(2,1)S(1)}, bf16[128,576]{0,1:T(8,128)(2,1)}, u32[]{:S(2)}) copy-start(bf16[128,576]{0,1:T(8,128)(2,1)} %param.8) | copy-start | bytes 442372
  16.4 14.8 %all-to-all-start = ((bf16[8,16,576]{2,1,0:T(8,128)(2,1)}), bf16[8,16,576]{2,1,0:T(8,128)(2,1)S(1)}, u32[]{:S(2)}, u32[]{:S(2)}) async-start(bf16[8,16,576]{2,1,0:T(8,128)(2,1)} %select_select_fusion), calls=%async_computation | async-start | bytes 327680 | tf_op jit(solution)/shard_map/all_to_all | solution.py:58
  23.7 29.5 %all-reduce.2.cloned.1.call-start = ((), (), s32[]{:S(2)}) async-start(), calls=%async_computation.1 | async-start | bytes 1835008 | tf_op jit(solution)/shard_map/psum | solution.py:70
  35.3 47.6 %all-gather.5.cloned.1.call-start = ((), (), s32[]{:S(2)}) async-start(), calls=%async_computation.3 | async-start | bytes 2064384 | tf_op jit(solution)/shard_map/all_gather | solution.py:83
  35.9 47.0 %copy-start.1 = (f32[3584]{0:T(1024)S(1)}, f32[3584]{0:T(1024)}, u32[]{:S(2)}) copy-start(f32[3584]{0:T(1024)} %param.12) | copy-start | bytes 43012
  35.9 150.4 %all-gather.3.cloned.1.call-start = ((), (), s32[]{:S(2)}) async-start(), calls=%async_computation.2 | async-start | bytes 7225344 | tf_op jit(solution)/shard_map/all_gather | solution.py:82
  82.9 2.8 %copy-start.2 = (bf16[32,1,256]{2,0,1:T(8,128)(2,1)S(1)}, bf16[32,1,256]{2,0,1:T(8,128)(2,1)}, u32[]{:S(2)}) copy-start(bf16[32,1,256]{2,0,1:T(8,128)(2,1)} %param.15) | copy-start | bytes 49156
Sparse Core Ops, SparseCore 0:
  35.5 17.6 all-reduce.1
Sparse Core Ops, SparseCore 1:
  38.0 44.8 all-gather.4
  85.0 101.3 all-gather.2
where the time goes:
time: 202 us; the launch traced here: 201 us
  waiting for transfers between devices  119 us (59%)
  blocking collectives  32.5 us (16%)
  between operations  15.7 us (8%)
  matrix products  12.2 us (6%)
  other arithmetic  10 us (5%)
  starting transfers between devices  7.37 us (4%)
  local copies, waits for them, and re-layouts  4.51 us (2%)
    all_gather x1, waiting for transfers between devices, per_device(): q_raw = add_rows(lax.all_gather(query_weight, 'seq', axis=0, tiled=True))  68.1 us
    all_gather x1, blocking collectives, per_device(): piece = lax.all_gather(context, 'seq', axis=0, tiled=True)  32.5 us
    all_gather x1, waiting for transfers between devices, per_device(): kv_raw = add_rows(lax.all_gather(keyval_weight, 'seq', axis=0, tiled=True))  26.4 us
    psum x1, waiting for transfers between devices, per_device(): pre_act = lax.psum(partial_pre, 'mdl')  16 us
    all_to_all x1, waiting for transfers between devices, per_device(): lax.all_to_all(outgoing, 'seq', split_axis=0, concat_axis=0, tiled=True)  7.28 us
    all_to_all x1, starting transfers between devices, per_device(): lax.all_to_all(outgoing, 'seq', split_axis=0, concat_axis=0, tiled=True)  7.25 us
    dot_general x2, matrix products, add_rows(): jnp.dot(normed, piece.reshape(piece.shape[0], -1), preferred_element_type...  6.07 us
    dot_general x1, matrix products, per_device(): jnp.dot(arrived_rows, proj_weight, preferred_element_type=jnp.float32)  4.09 us
  transfers between devices with their start and end apart: 4, of which 4 were waited for; matrix products, arithmetic and copies ran while one was open for 3% of the time, Pallas kernels for 0%

commit v1 on v0

--- a/solution.py
+++ b/solution.py
@@ -1,8 +1,12 @@
+import functools
 import math
 
 import jax
 import jax.numpy as jnp
+import numpy as np
 from jax import lax
+from jax.experimental import pallas as pl
+from jax.experimental.pallas import tpu as pltpu
 from jax.sharding import PartitionSpec as P
 
 theta_base = 1000000.0
@@ -24,7 +28,7 @@
     return head_rows * cosine + turned * sine_part
 
 
-def per_device(
+def plain_plan(
     vis_tokens,
     merge_target,
     merged_counts,
@@ -164,6 +168,422 @@
     return (attended, fresh.reshape(new_dev, 1, kv_heads, 2 * head_dim))
 
 
+MESH = pl.DeviceIdType.MESH
+XS = 2
+
+
+def fused_kernel(
+    n,
+    vis_ref,
+    target_ref,
+    counts_ref,
+    gain_ref,
+    proj_hbm,
+    wq_hbm,
+    wkv_hbm,
+    cache_hbm,
+    cos_hbm,
+    sin_hbm,
+    attn_ref,
+    newkv_ref,
+    proj,
+    wq,
+    wkv,
+    cos_t,
+    sin_t,
+    cache_all,
+    packed,
+    incoming,
+    pre,
+    pre_recv,
+    act,
+    norm_send,
+    norm_all,
+    part_kv,
+    part_q,
+    xsend_kv,
+    xrecv_kv,
+    zsend_kv,
+    zrecv_kv,
+    xsend_q,
+    xrecv_q,
+    zsend_q,
+    zrecv_q,
+    fresh_all,
+    q_rows,
+    load_sem,
+    s_cache,
+    r_cache,
+    s_tok,
+    r_tok,
+    s_pre,
+    r_pre,
+    s_norm,
+    r_norm,
+    s_fwd,
+    r_fwd,
+    s_x,
+    r_x,
+    s_z,
+    r_z,
+    s_fresh,
+    r_fresh,
+):
+    s = lax.axis_index("seq")
+    m = lax.axis_index("mdl")
+    zs = n // XS
+    z, x = s // XS, s % XS
+    mate = {"mdl": 1 - m}
+    peers = [(s + k) % n for k in range(n)]
+
+    def send(src, dst, ssem, rsem, device):
+        copy = pltpu.make_async_remote_copy(
+            src_ref=src,
+            dst_ref=dst,
+            send_sem=ssem,
+            recv_sem=rsem,
+            device_id=device,
+            device_id_type=MESH,
+        )
+        copy.start()
+        return copy
+
+    barrier = pltpu.get_barrier_semaphore()
+    for k in range(1, n):
+        pl.semaphore_signal(barrier, inc=1, device_id={"seq": peers[k]}, device_id_type=MESH)
+    pl.semaphore_signal(barrier, inc=1, device_id=mate, device_id_type=MESH)
+
+    loads = []
+    for at, (src, dst) in enumerate(
+        (
+            (cache_hbm, cache_all.at[s]),
+            (proj_hbm, proj),
+            (wkv_hbm, wkv),
+            (wq_hbm, wq),
+            (cos_hbm.at[s], cos_t),
+            (sin_hbm.at[s], sin_t),
+        )
+    ):
+        copy = pltpu.make_async_copy(src, dst, load_sem.at[at])
+        copy.start()
+        loads.append(copy)
+
+    toks = vis_ref.shape[0]
+    cap = packed.shape[1]
+    slots = n * cap
+    new_dev = toks // 2
+    prefix = []
+    running = jnp.int32(0)
+    here = jnp.int32(0)
+    for i in range(n):
+        prefix.append(running)
+        here = jnp.where(s == i, running, here)
+        running = running + counts_ref[i]
+    slot = lax.broadcasted_iota(jnp.int32, (slots, toks), 0)
+    local_row = ((slot // cap - here) & (n - 1)) + (slot % cap) * n
+    chosen = jnp.where(local_row == target_ref[...], 1.0, 0.0)
+    sizes = jnp.sum(chosen, axis=1, keepdims=True)
+    summed = jnp.dot(
+        chosen.astype(jnp.bfloat16), vis_ref[...], preferred_element_type=jnp.float32
+    )
+    merged = (summed / jnp.where(sizes > 0.0, sizes, 1.0)).astype(jnp.bfloat16)
+    packed[...] = merged.reshape(packed.shape)
+
+    pl.semaphore_wait(barrier, n)
+    tok_copies = [
+        send(packed.at[peers[k]], incoming.at[s], s_tok.at[k], r_tok.at[k], {"seq": peers[k]})
+        for k in range(1, n)
+    ]
+    loads[0].wait()
+    cache_copies = [
+        send(cache_all.at[s], cache_all.at[s], s_cache.at[k], r_cache.at[k], {"seq": peers[k]})
+        for k in range(1, n)
+    ]
+    incoming[s] = packed[s]
+
+    column = lax.broadcasted_iota(jnp.int32, (new_dev, slots), 1)
+    source = column // cap
+    starts = jnp.zeros_like(column)
+    ends = jnp.zeros_like(column)
+    for i in range(n):
+        starts = jnp.where(source == i, prefix[i], starts)
+        ends = jnp.where(source == i, prefix[i] + counts_ref[i], ends)
+    global_row = starts + ((s - starts) & (n - 1)) + (column % cap) * n
+    goal = jnp.where(global_row < ends, global_row // n, -1)
+    placing = jnp.where(
+        goal == lax.broadcasted_iota(jnp.int32, (new_dev, slots), 0), 1.0, 0.0
+    ).astype(jnp.bfloat16)
+    loads[1].wait()
+    for copy in tok_copies:
+        copy.wait()
+    rows = jnp.dot(
+        placing,
+        incoming[...].reshape(slots, incoming.shape[2]),
+        preferred_element_type=jnp.float32,
+    ).astype(jnp.bfloat16)
+
+    width = proj.shape[1]
+    half = new_dev // 2
+    step = 512
+    mine = pl.ds(pl.multiple_of(m * half, half), half)
+    other = pl.ds(pl.multiple_of((1 - m) * half, half), half)
+    pre_copies = []
+    for c in range(width // step):
+        cols = pl.ds(c * step, step)
+        pre[c] = jnp.dot(rows, proj[:, cols], preferred_element_type=jnp.float32)
+        pre_copies.append(
+            send(pre.at[c, other], pre_recv.at[c], s_pre.at[c], r_pre.at[c], mate)
+        )
+    square = jnp.zeros((half, step), jnp.float32)
+    for c in range(width // step):
+        pre_copies[c].wait()
+        value = pre[c, mine] + pre_recv[c]
+        value = 0.5 * value * (1.0 + lax.erf(value * (1.0 / math.sqrt(2.0))))
+        square = square + value * value
+        act[:, pl.ds(c * step, step)] = value
+    mean = jnp.sum(square, axis=1, keepdims=True) / width
+    inv_rms = lax.rsqrt(mean + norm_eps)
+    normed = (act[...] * inv_rms * gain_ref[...]).astype(jnp.bfloat16)
+    depth = width // n
+    for d in range(n):
+        norm_send[d] = normed[:, d * depth : (d + 1) * depth]
+    norm_copies = [
+        send(norm_send.at[peers[k]], norm_all.at[s, m], s_norm.at[k], r_norm.at[k], {"seq": peers[k]})
+        for k in range(1, n)
+    ]
+    norm_all[s, m] = norm_send[s]
+    forwards = [send(norm_all.at[s, m], norm_all.at[s, m], s_fwd.at[0], r_fwd.at[0], mate)]
+    for k in range(1, n):
+        norm_copies[k - 1].wait()
+        came = norm_all.at[(s + n - k) % n, m]
+        forwards.append(send(came, came, s_fwd.at[k], r_fwd.at[k], mate))
+    loads[2].wait()
+    loads[3].wait()
+    for copy in forwards:
+        copy.wait()
+
+    lhs = norm_all[...].reshape(n * new_dev, depth)
+    x_copies = {}
+    order = [(z + k) % zs for k in range(1, zs)] + [z]
+    for which, weight, part, xsend, xrecv in (
+        (0, wkv, part_kv, xsend_kv, xrecv_kv),
+        (1, wq, part_q, xsend_q, xrecv_q),
+    ):
+        part[...] = jnp.dot(lhs, weight[...], preferred_element_type=jnp.float32).reshape(
+            part.shape
+        )
+        for k, zt in enumerate(order):
+            xsend[k] = part[zt * XS + 1 - x].astype(jnp.bfloat16)
+            x_copies[which, k] = send(
+                xsend.at[k],
+                xrecv.at[k],
+                s_x.at[which, k],
+                r_x.at[which, k],
+                {"seq": z * XS + 1 - x},
+            )
+
+    def along_z(which, part, xrecv, zsend, zrecv):
+        copies = []
+        for k in range(1, zs):
+            zt = order[k - 1]
+            x_copies[which, k - 1].wait()
+            zsend[k - 1] = (
+                part[zt * XS + x] + xrecv[k - 1].astype(jnp.float32)
+            ).astype(jnp.bfloat16)
+            copies.append(
+                send(
+                    zsend.at[k - 1],
+                    zrecv.at[k - 1],
+                    s_z.at[which, k - 1],
+                    r_z.at[which, k - 1],
+                    {"seq": zt * XS + x},
+                )
+            )
+        x_copies[which, zs - 1].wait()
+        return part[s] + xrecv[zs - 1].astype(jnp.float32), copies
+
+    def finish(total, copies, zrecv):
+        for k, copy in enumerate(copies):
+            copy.wait()
+            total = total + zrecv[k].astype(jnp.float32)
+        return total
+
+    head = cos_t.shape[1]
+    loads[4].wait()
+    loads[5].wait()
+    cosine, sine = cos_t[...], sin_t[...]
+
+    def turn(value):
+        return value * cosine + pltpu.roll(value, head // 2, 1) * sine
+
+    total, copies = along_z(0, part_kv, xrecv_kv, zsend_kv, zrecv_kv)
+    total = finish(total, copies, zrecv_kv)
+    fresh = jnp.concatenate([turn(total[:, :head]), total[:, head:]], axis=1).astype(jnp.bfloat16)
+    fresh_all[s] = fresh
+    newkv_ref[...] = fresh
+    fresh_copies = [
+        send(fresh_all.at[s], fresh_all.at[s], s_fresh.at[k], r_fresh.at[k], {"seq": peers[k]})
+        for k in range(1, n)
+    ]
+    total, copies = along_z(1, part_q, xrecv_q, zsend_q, zrecv_q)
+    total = finish(total, copies, zrecv_q)
+    heads = total.shape[1] // head
+    for h in range(heads):
+        q_rows[pl.ds(h * new_dev, new_dev), :] = turn(
+            total[:, h * head : (h + 1) * head]
+        ).astype(jnp.bfloat16)
+    for copy in cache_copies:
+        copy.wait()
+    for copy in fresh_copies:
+        copy.wait()
+
+    kept = cache_all.shape[0] * cache_all.shape[1]
+    old = cache_all[...].reshape(kept, 2 * head)
+    new = fresh_all[...].reshape(n * new_dev, 2 * head)
+    queries = q_rows[...]
+    contract = (((1,), (1,)), ((), ()))
+    scale = 1.0 / math.sqrt(head)
+    old_score = (
+        lax.dot_general(queries, old[:, :head], contract, preferred_element_type=jnp.float32) * scale
+    )
+    new_score = (
+        lax.dot_general(queries, new[:, :head], contract, preferred_element_type=jnp.float32) * scale
+    )
+    lanes = heads * new_dev
+    key_at = lax.broadcasted_iota(jnp.int32, (lanes, n * new_dev), 1)
+    query_at = lax.broadcasted_iota(jnp.int32, (lanes, n * new_dev), 0)
+    visible = (key_at % new_dev) * n + key_at // new_dev <= (query_at % new_dev) * n + s
+    new_score = jnp.where(visible, new_score, mask_fill)
+    top = jnp.maximum(
+        jnp.max(old_score, axis=1, keepdims=True), jnp.max(new_score, axis=1, keepdims=True)
+    )
+    old_weight = jnp.exp(old_score - top)
+    new_weight = jnp.where(visible, jnp.exp(new_score - top), 0.0)
+    totals = jnp.sum(old_weight, axis=1, keepdims=True) + jnp.sum(new_weight, axis=1, keepdims=True)
+    mixed = jnp.dot(
+        old_weight.astype(jnp.bfloat16), old[:, head:], preferred_element_type=jnp.float32
+    ) + jnp.dot(new_weight.astype(jnp.bfloat16), new[:, head:], preferred_element_type=jnp.float32)
+    attended = (mixed / totals).astype(jnp.bfloat16)
+    for h in range(heads):
+        attn_ref[:, pl.ds(h * head, head)] = attended[h * new_dev : (h + 1) * new_dev]
+
+
+def fused_plan(
+    vis_tokens,
+    merge_target,
+    merged_counts,
+    proj_weight,
+    norm_gain,
+    query_weight,
+    keyval_weight,
+    cache_kv,
+):
+    n = lax.axis_size("seq")
+    zs = n // XS
+    toks, feat = vis_tokens.shape
+    new_dev = toks // 2
+    half = new_dev // 2
+    cap = (new_dev + 3 * (new_dev // 3) + n - 1) // n
+    width = proj_weight.shape[1]
+    depth, qcols = query_weight.shape
+    kvcols = keyval_weight.shape[2]
+    head = kvcols // 2
+    cached = cache_kv.shape[0]
+    pos = (
+        cached * n + np.arange(new_dev, dtype=np.float32)[None, :] * n
+        + np.arange(n, dtype=np.float32)[:, None]
+    ).astype(np.float32)
+    freq = np.power(
+        np.float32(theta_base), np.float32(-2.0) * np.arange(head // 2, dtype=np.float32) / np.float32(head)
+    ).astype(np.float32)
+    angles = (pos[:, :, None] * freq[None, None, :]).astype(np.float64)
+    cos_table = np.concatenate([np.cos(angles)] * 2, axis=-1).astype(np.float32)
+    sin_table = np.concatenate([-np.sin(angles), np.sin(angles)], axis=-1).astype(np.float32)
+    bf, f32 = jnp.bfloat16, jnp.float32
+    chunks = width // 512
+    vm, dma = pltpu.VMEM, pltpu.SemaphoreType.DMA
+    scratch = [
+        vm((feat, width), bf),
+        vm((depth, qcols), bf),
+        vm((depth, kvcols), bf),
+        vm((new_dev, head), f32),
+        vm((new_dev, head), f32),
+        vm((n, cached, kvcols), bf),
+        vm((n, cap, feat), bf),
+        vm((n, cap, feat), bf),
+        vm((chunks, new_dev, 512), f32),
+        vm((chunks, half, 512), f32),
+        vm((half, width), f32),
+        vm((n, half, depth), bf),
+        vm((n, 2, half, depth), bf),
+        vm((n, new_dev, kvcols), f32),
+        vm((n, new_dev, qcols), f32),
+        vm((zs, new_dev, kvcols), bf),
+        vm((zs, new_dev, kvcols), bf),
+        vm((zs - 1, new_dev, kvcols), bf),
+        vm((zs - 1, new_dev, kvcols), bf),
+        vm((zs, new_dev, qcols), bf),
+        vm((zs, new_dev, qcols), bf),
+        vm((zs - 1, new_dev, qcols), bf),
+        vm((zs - 1, new_dev, qcols), bf),
+        vm((n, new_dev, kvcols), bf),
+        vm((qcols // head * new_dev, head), bf),
+        dma((6,)),
+        dma((n,)),
+        dma((n,)),
+        dma((n,)),
+        dma((n,)),
+        dma((chunks,)),
+        dma((chunks,)),
+        dma((n,)),
+        dma((n,)),
+        dma((n,)),
+        dma((n,)),
+        dma((2, zs)),
+        dma((2, zs)),
+        dma((2, zs)),
+        dma((2, zs)),
+        dma((n,)),
+        dma((n,)),
+    ]
+    in_vmem = pl.BlockSpec(memory_space=pltpu.VMEM)
+    anywhere = pl.BlockSpec(memory_space=pl.ANY)
+    attended, fresh = pl.pallas_call(
+        functools.partial(fused_kernel, n),
+        out_shape=(
+            jax.ShapeDtypeStruct((new_dev, qcols), bf),
+            jax.ShapeDtypeStruct((new_dev, kvcols), bf),
+        ),
+        in_specs=[
+            in_vmem,
+            in_vmem,
+            pl.BlockSpec(memory_space=pltpu.SMEM),
+            in_vmem,
+        ]
+        + [anywhere] * 6,
+        out_specs=(in_vmem, in_vmem),
+        scratch_shapes=scratch,
+        compiler_params=pltpu.CompilerParams(
+            collective_id=0, has_side_effects=True, vmem_limit_bytes=48 * 1024 * 1024
+        ),
+    )(
+        vis_tokens,
+        merge_target.reshape(1, toks),
+        merged_counts,
+        norm_gain.reshape(1, width),
+        proj_weight,
+        query_weight,
+        keyval_weight.reshape(depth, kvcols),
+        cache_kv.reshape(cached, kvcols),
+        jnp.asarray(cos_table),
+        jnp.asarray(sin_table),
+    )
+    return (
+        attended.reshape(new_dev, 1, qcols),
+        fresh.reshape(new_dev, 1, keyval_weight.shape[1], kvcols),
+    )
+
+
 def solution(mesh):
     placed = (
         P(("grp", "seq"), "mdl"),
@@ -175,6 +595,7 @@
         P("seq", "mdl", None),
         P(("grp", "seq"), "mdl", None),
     )
+    per_device = fused_plan if mesh.shape["seq"] == 8 else plain_plan
     return jax.shard_map(
         per_device,
         mesh=mesh,

time: 202 us -> 62.3 us (0.31)
  waiting for transfers between devices: 119 us -> 0 us
  Pallas kernels: 0 us -> 50 us
  blocking collectives: 32.5 us -> 0 us
  between operations: 15.7 us -> 0.66 us
  matrix products: 12.2 us -> 0 us
  other arithmetic: 10 us -> 0 us
  starting transfers between devices: 7.37 us -> 0 us
  local copies, waits for them, and re-layouts: 4.51 us -> 11.2 us
    all_gather x2 -> x0, waiting for transfers between devices: 94.5 us -> none  [the longest x1 68.1 us: per_device(): q_raw = add_rows(lax.all_gather(query_weight, 'seq', axis=0, tiled=True))]
    pallas_call x0 -> x1, Pallas kernels: none -> 50 us  [fused_plan(): pl.pallas_call(functools.partial(fused_kernel, n), out_shape=(jax.ShapeDt...]
    all_gather x1 -> x0, blocking collectives: 32.5 us -> none  [per_device(): piece = lax.all_gather(context, 'seq', axis=0, tiled=True)]
    psum x1 -> x0, waiting for transfers between devices: 16 us -> none  [per_device(): pre_act = lax.psum(partial_pre, 'mdl')]
    dot_general x6 -> x0, matrix products: 12.2 us -> none  [the longest x2 6.07 us: add_rows(): jnp.dot(normed, piece.reshape(piece.shape[0], -1), preferred_element_type...]
    unnamed x6 -> x19, local copies, waits for them, and re-layouts: 0.02 us -> 10.5 us
    all_to_all x1 -> x0, waiting for transfers between devices: 7.28 us -> none  [per_device(): lax.all_to_all(outgoing, 'seq', split_axis=0, concat_axis=0, tiled=True)]
    all_to_all x1 -> x0, starting transfers between devices: 7.25 us -> none  [per_device(): lax.all_to_all(outgoing, 'seq', split_axis=0, concat_axis=0, tiled=True)]
  transfers between devices with their start and end apart: 4 -> 0, of which waited for: 4 -> 0; matrix products, arithmetic and copies ran while one was open for 3% -> 0% of each run, Pallas kernels for 0% -> 0%
where the time goes in v1:
time: 62.3 us; the launch traced here: 61.9 us
  Pallas kernels  50 us (80%)
  local copies, waits for them, and re-layouts  11.2 us (18%)
  between operations  0.66 us (1%)
    pallas_call x1, Pallas kernels, fused_plan(): pl.pallas_call(functools.partial(fused_kernel, n), out_shape=(jax.ShapeDt...  50 us
    unnamed x19, local copies, waits for them, and re-layouts  10.5 us

profile of v1, /device:TPU:0, one launch (start us, length us, event | category | flops | bytes accessed | tf_op | source)
XLA Modules:
  0.0 61.9 jit_solution(5973365506840709200)
XLA Ops:
  0.6 0.7 %reshape.23.gain_ref = f32[1,3584]{1,0:T(1,128)S(1)} reshape(f32[3584]{0:T(1024)} %param.14) | data formatting | bytes 28672 | tf_op jit(solution)/shard_map/reshape | solution.py:573
  1.4 1.1 %copy.12.vis_ref = bf16[128,576]{1,0:T(8,128)(2,1)S(1)} copy(bf16[128,576]{0,1:T(8,128)(2,1)} %param.10) | data formatting | bytes 294912 | tf_op args[0]
  2.4 0.0 copy-start
  2.4 2.2 %copy-done = bf16[576,3584]{1,0:T(8,128)(2,1)S(1)} copy-done((bf16[576,3584]{1,0:T(8,128)(2,1)S(1)}, bf16[576,3584]{1,0:T(8,128)(2,1)}, u32[]{:S(2)}) %copy-start) | copy-done | bytes 4128792
  4.6 0.0 copy-start.1
  4.6 1.1 %copy-done.1 = bf16[448,896]{1,0:T(8,128)(2,1)S(1)} copy-done((bf16[448,896]{1,0:T(8,128)(2,1)S(1)}, bf16[448,896]{1,0:T(8,128)(2,1)}, u32[]{:S(2)}) %copy-start.1) | copy-done | bytes 802840
  5.7 0.0 copy-start.2
  5.7 0.9 %copy-done.2 = f32[8,64,128]{2,1,0:T(8,128)S(1)} copy-done((f32[8,64,128]{2,1,0:T(8,128)S(1)}, f32[8,64,128]{2,1,0:T(8,128)}, u32[]{:S(2)}) %copy-start.2) | copy-done | bytes 262168
  6.7 0.0 copy-start.3
  6.7 0.9 %copy-done.3 = f32[8,64,128]{2,1,0:T(8,128)S(1)} copy-done((f32[8,64,128]{2,1,0:T(8,128)S(1)}, f32[8,64,128]{2,1,0:T(8,128)}, u32[]{:S(2)}) %copy-start.3) | copy-done | bytes 262168
  7.6 0.0 copy-start.4
  7.6 0.9 %copy-done.4 = bf16[448,1,256]{2,0,1:T(8,128)(2,1)S(1)} copy-done((bf16[448,1,256]{2,0,1:T(8,128)(2,1)S(1)}, bf16[448,1,256]{2,0,1:T(8,128)(2,1)}, u32[]{:S(2)}) %copy-start.4) | copy-done | bytes 229400
  8.6 0.0 copy-start.5
  8.6 0.7 %copy-done.5 = bf16[32,1,256]{2,0,1:T(8,128)(2,1)S(1)} copy-done((bf16[32,1,256]{2,0,1:T(8,128)(2,1)S(1)}, bf16[32,1,256]{2,0,1:T(8,128)(2,1)}, u32[]{:S(2)}) %copy-start.5) | copy-done | bytes 16408
  9.3 0.0 copy-start.6
  9.3 0.7 %copy-done.6 = s32[128]{0:T(128)S(1)} copy-done((s32[128]{0:T(128)S(1)}, s32[128]{0:T(128)}, u32[]{:S(2)}) %copy-start.6) | copy-done | bytes 536
  10.0 0.0 copy-start.7
  10.0 0.7 %copy-done.7 = s32[8]{0:T(128)S(1)} copy-done((s32[8]{0:T(128)S(1)}, s32[8]{0:T(128)}, u32[]{:S(2)}) %copy-start.7) | copy-done | bytes 56
  10.6 50.0 %shard_map.113 = (bf16[64,896]{1,0:T(8,128)(2,1)S(1)}, bf16[64,256]{1,0:T(8,128)(2,1)S(1)}) custom-call(bf16[128,576]{1,0:T(8,128)(2,1)S(1)} %copy.12.vis_ref, s32[1,128]{1,0:T(1,128)S(1)} %bitcast.9, s32[8]{0:T(128)S(1)} %copy-done.7, f32[1,3584]{1,0:T(1,128)S(1)} %reshape.23.gain_ref, bf16[576,3584]{1,0:T(8,128)(2,1)S(1)} %copy-done, ...), custom_call_target="tpu_custom_call" | custom-call | tf_op jit(solution)/shard_map/pallas_call | solution.py:551
  60.6 0.6 %copy.15 = bf16[64,1,896]{2,0,1:T(8,128)(2,1)} copy(bf16[64,1,896]{2,0,1:T(8,128)(2,1)S(1)} %bitcast.6) | data formatting | bytes 229376
  61.3 0.6 copy.16
Async XLA Ops:
  2.4 2.2 %copy-start = (bf16[576,3584]{1,0:T(8,128)(2,1)S(1)}, bf16[576,3584]{1,0:T(8,128)(2,1)}, u32[]{:S(2)}) copy-start(bf16[576,3584]{1,0:T(8,128)(2,1)} %proj_hbm.1) | copy-start | bytes 12386308
  4.6 1.1 %copy-start.1 = (bf16[448,896]{1,0:T(8,128)(2,1)S(1)}, bf16[448,896]{1,0:T(8,128)(2,1)}, u32[]{:S(2)}) copy-start(bf16[448,896]{1,0:T(8,128)(2,1)} %wq_hbm.1) | copy-start | bytes 2408452
  5.7 0.9 %copy-start.2 = (f32[8,64,128]{2,1,0:T(8,128)S(1)}, f32[8,64,128]{2,1,0:T(8,128)}, u32[]{:S(2)}) copy-start(f32[8,64,128]{2,1,0:T(8,128)} %constant.5.clone.sin_hbm) | copy-start | bytes 786436
  6.7 0.9 %copy-start.3 = (f32[8,64,128]{2,1,0:T(8,128)S(1)}, f32[8,64,128]{2,1,0:T(8,128)}, u32[]{:S(2)}) copy-start(f32[8,64,128]{2,1,0:T(8,128)} %constant.4.clone.cos_hbm) | copy-start | bytes 786436
  7.6 0.9 %copy-start.4 = (bf16[448,1,256]{2,0,1:T(8,128)(2,1)S(1)}, bf16[448,1,256]{2,0,1:T(8,128)(2,1)}, u32[]{:S(2)}) copy-start(bf16[448,1,256]{2,0,1:T(8,128)(2,1)} %param.16) | copy-start | bytes 688132
  8.6 0.7 %copy-start.5 = (bf16[32,1,256]{2,0,1:T(8,128)(2,1)S(1)}, bf16[32,1,256]{2,0,1:T(8,128)(2,1)}, u32[]{:S(2)}) copy-start(bf16[32,1,256]{2,0,1:T(8,128)(2,1)} %param.17) | copy-start | bytes 49156
  9.3 0.7 %copy-start.6 = (s32[128]{0:T(128)S(1)}, s32[128]{0:T(128)}, u32[]{:S(2)}) copy-start(s32[128]{0:T(128)} %param.11) | copy-start | bytes 1540
  10.0 0.7 %copy-start.7 = (s32[8]{0:T(128)S(1)}, s32[8]{0:T(128)}, u32[]{:S(2)}) copy-start(s32[8]{0:T(128)} %counts_ref.1) | copy-start | bytes 100

commit v2 on v1

--- a/solution.py
+++ b/solution.py
@@ -174,10 +174,10 @@
 
 def fused_kernel(
     n,
-    vis_ref,
-    target_ref,
-    counts_ref,
-    gain_ref,
+    vis_hbm,
+    target_hbm,
+    counts_hbm,
+    gain_hbm,
     proj_hbm,
     wq_hbm,
     wkv_hbm,
@@ -186,6 +186,10 @@
     sin_hbm,
     attn_ref,
     newkv_ref,
+    vis_ref,
+    target_ref,
+    counts_ref,
+    gain_ref,
     proj,
     wq,
     wkv,
@@ -201,12 +205,8 @@
     norm_all,
     part_kv,
     part_q,
-    xsend_kv,
-    xrecv_kv,
     zsend_kv,
     zrecv_kv,
-    xsend_q,
-    xrecv_q,
     zsend_q,
     zrecv_q,
     fresh_all,
@@ -222,8 +222,10 @@
     r_norm,
     s_fwd,
     r_fwd,
-    s_x,
-    r_x,
+    s_w,
+    r_w,
+    s_y,
+    r_y,
     s_z,
     r_z,
     s_fresh,
@@ -233,7 +235,10 @@
     m = lax.axis_index("mdl")
     zs = n // XS
     z, x = s // XS, s % XS
+    g = lax.axis_index("grp")
     mate = {"mdl": 1 - m}
+    beside_x = {"seq": z * XS + 1 - x}
+    beside_y = {"grp": 1 - g}
     peers = [(s + k) % n for k in range(n)]
 
     def send(src, dst, ssem, rsem, device):
@@ -252,26 +257,32 @@
     for k in range(1, n):
         pl.semaphore_signal(barrier, inc=1, device_id={"seq": peers[k]}, device_id_type=MESH)
     pl.semaphore_signal(barrier, inc=1, device_id=mate, device_id_type=MESH)
+    pl.semaphore_signal(barrier, inc=1, device_id=beside_y, device_id_type=MESH)
 
     loads = []
     for at, (src, dst) in enumerate(
         (
+            (counts_hbm, counts_ref),
+            (target_hbm, target_ref),
+            (vis_hbm, vis_ref),
             (cache_hbm, cache_all.at[s]),
+            (wkv_hbm, wkv.at[x]),
+            (wq_hbm, wq.at[x]),
             (proj_hbm, proj),
-            (wkv_hbm, wkv),
-            (wq_hbm, wq),
             (cos_hbm.at[s], cos_t),
             (sin_hbm.at[s], sin_t),
+            (gain_hbm, gain_ref),
         )
     ):
         copy = pltpu.make_async_copy(src, dst, load_sem.at[at])
         copy.start()
         loads.append(copy)
 
-    toks = vis_ref.shape[0]
+    toks = vis_ref.shape[1]
     cap = packed.shape[1]
     slots = n * cap
     new_dev = toks // 2
+    loads[0].wait()
     prefix = []
     running = jnp.int32(0)
     here = jnp.int32(0)
@@ -281,20 +292,44 @@
         running = running + counts_ref[i]
     slot = lax.broadcasted_iota(jnp.int32, (slots, toks), 0)
     local_row = ((slot // cap - here) & (n - 1)) + (slot % cap) * n
+    loads[1].wait()
     chosen = jnp.where(local_row == target_ref[...], 1.0, 0.0)
     sizes = jnp.sum(chosen, axis=1, keepdims=True)
-    summed = jnp.dot(
-        chosen.astype(jnp.bfloat16), vis_ref[...], preferred_element_type=jnp.float32
+    loads[2].wait()
+    contract = (((1,), (1,)), ((), ()))
+    summed = lax.dot_general(
+        chosen.astype(jnp.bfloat16), vis_ref[...], contract, preferred_element_type=jnp.float32
     )
     merged = (summed / jnp.where(sizes > 0.0, sizes, 1.0)).astype(jnp.bfloat16)
     packed[...] = merged.reshape(packed.shape)
 
-    pl.semaphore_wait(barrier, n)
+    pl.semaphore_wait(barrier, n + 1)
     tok_copies = [
         send(packed.at[peers[k]], incoming.at[s], s_tok.at[k], r_tok.at[k], {"seq": peers[k]})
         for k in range(1, n)
     ]
-    loads[0].wait()
+    depth = wq.shape[1]
+    part_rows = depth // 4
+    loads[4].wait()
+    loads[5].wait()
+    pieces = []
+    for c in range(2):
+        at = pl.ds(pl.multiple_of((g * 2 + c) * part_rows, 16), part_rows)
+        for which, weight in enumerate((wkv, wq)):
+            pieces.append((weight.at[x, at], weight.at[1 - x, at]))
+    straight = [
+        send(src, src, s_w.at[at], r_w.at[at], beside_x) for at, (src, _) in enumerate(pieces)
+    ]
+
+    def pass_on(which):
+        copies = []
+        for at in which:
+            straight[at].wait()
+            dst = pieces[at][1]
+            copies.append(send(dst, dst, s_y.at[at], r_y.at[at], beside_y))
+        return copies
+
+    loads[3].wait()
     cache_copies = [
         send(cache_all.at[s], cache_all.at[s], s_cache.at[k], r_cache.at[k], {"seq": peers[k]})
         for k in range(1, n)
@@ -313,7 +348,7 @@
     placing = jnp.where(
         goal == lax.broadcasted_iota(jnp.int32, (new_dev, slots), 0), 1.0, 0.0
     ).astype(jnp.bfloat16)
-    loads[1].wait()
+    loads[6].wait()
     for copy in tok_copies:
         copy.wait()
     rows = jnp.dot(
@@ -343,64 +378,65 @@
         act[:, pl.ds(c * step, step)] = value
     mean = jnp.sum(square, axis=1, keepdims=True) / width
     inv_rms = lax.rsqrt(mean + norm_eps)
-    normed = (act[...] * inv_rms * gain_ref[...]).astype(jnp.bfloat16)
-    depth = width // n
-    for d in range(n):
-        norm_send[d] = normed[:, d * depth : (d + 1) * depth]
-    norm_copies = [
-        send(norm_send.at[peers[k]], norm_all.at[s, m], s_norm.at[k], r_norm.at[k], {"seq": peers[k]})
-        for k in range(1, n)
-    ]
-    norm_all[s, m] = norm_send[s]
-    forwards = [send(norm_all.at[s, m], norm_all.at[s, m], s_fwd.at[0], r_fwd.at[0], mate)]
-    for k in range(1, n):
+    loads[9].wait()
+    lane = gain_ref.shape[1]
+    normed = jnp.concatenate(
+        [
+            (act[:, pl.ds(j * lane, lane)] * inv_rms * gain_ref[pl.ds(j, 1), :]).astype(
+                jnp.bfloat16
+            )
+            for j in range(width // lane)
+        ],
+        axis=1,
+    )
+    wide = width // zs
+    for d in range(zs):
+        norm_send[d] = normed[:, d * wide : (d + 1) * wide]
+    norm_copies = []
+    for k in range(1, zs):
+        zt = (z + k) % zs
+        norm_copies.append(
+            send(
+                norm_send.at[zt],
+                norm_all.at[z, m],
+                s_norm.at[k],
+                r_norm.at[k],
+                {"seq": zt * XS + x},
+            )
+        )
+    norm_all[z, m] = norm_send[z]
+    forwards = [send(norm_all.at[z, m], norm_all.at[z, m], s_fwd.at[0], r_fwd.at[0], mate)]
+    crossing = pass_on((0, 1))
+    for k in range(1, zs):
         norm_copies[k - 1].wait()
-        came = norm_all.at[(s + n - k) % n, m]
+        came = norm_all.at[(z + zs - k) % zs, m]
         forwards.append(send(came, came, s_fwd.at[k], r_fwd.at[k], mate))
-    loads[2].wait()
-    loads[3].wait()
+    crossing = crossing + pass_on((2, 3))
     for copy in forwards:
         copy.wait()
-
-    lhs = norm_all[...].reshape(n * new_dev, depth)
-    x_copies = {}
-    order = [(z + k) % zs for k in range(1, zs)] + [z]
-    for which, weight, part, xsend, xrecv in (
-        (0, wkv, part_kv, xsend_kv, xrecv_kv),
-        (1, wq, part_q, xsend_q, xrecv_q),
-    ):
-        part[...] = jnp.dot(lhs, weight[...], preferred_element_type=jnp.float32).reshape(
-            part.shape
-        )
+    for copy in crossing:
+        copy.wait()
+
+    lhs = norm_all[...].reshape(zs * new_dev, wide)
+    order = [(z + k) % zs for k in range(1, zs)]
+
+    def along_z(which, weight, part, zsend, zrecv):
+        part[...] = jnp.dot(
+            lhs, weight[...].reshape(wide, weight.shape[2]), preferred_element_type=jnp.float32
+        ).reshape(part.shape)
+        copies = []
         for k, zt in enumerate(order):
-            xsend[k] = part[zt * XS + 1 - x].astype(jnp.bfloat16)
-            x_copies[which, k] = send(
-                xsend.at[k],
-                xrecv.at[k],
-                s_x.at[which, k],
-                r_x.at[which, k],
-                {"seq": z * XS + 1 - x},
-            )
-
-    def along_z(which, part, xrecv, zsend, zrecv):
-        copies = []
-        for k in range(1, zs):
-            zt = order[k - 1]
-            x_copies[which, k - 1].wait()
-            zsend[k - 1] = (
-                part[zt * XS + x] + xrecv[k - 1].astype(jnp.float32)
-            ).astype(jnp.bfloat16)
+            zsend[k] = part[zt].astype(jnp.bfloat16)
             copies.append(
                 send(
-                    zsend.at[k - 1],
-                    zrecv.at[k - 1],
-                    s_z.at[which, k - 1],
-                    r_z.at[which, k - 1],
+                    zsend.at[k],
+                    zrecv.at[k],
+                    s_z.at[which, k],
+                    r_z.at[which, k],
                     {"seq": zt * XS + x},
                 )
             )
-        x_copies[which, zs - 1].wait()
-        return part[s] + xrecv[zs - 1].astype(jnp.float32), copies
+        return part[z], copies
 
     def finish(total, copies, zrecv):
         for k, copy in enumerate(copies):
@@ -409,15 +445,16 @@
         return total
 
     head = cos_t.shape[1]
-    loads[4].wait()
-    loads[5].wait()
+    kv_own, kv_copies = along_z(0, wkv, part_kv, zsend_kv, zrecv_kv)
+    q_own, q_copies = along_z(1, wq, part_q, zsend_q, zrecv_q)
+    loads[7].wait()
+    loads[8].wait()
     cosine, sine = cos_t[...], sin_t[...]
 
     def turn(value):
         return value * cosine + pltpu.roll(value, head // 2, 1) * sine
 
-    total, copies = along_z(0, part_kv, xrecv_kv, zsend_kv, zrecv_kv)
-    total = finish(total, copies, zrecv_kv)
+    total = finish(kv_own, kv_copies, zrecv_kv)
     fresh = jnp.concatenate([turn(total[:, :head]), total[:, head:]], axis=1).astype(jnp.bfloat16)
     fresh_all[s] = fresh
     newkv_ref[...] = fresh
@@ -425,8 +462,7 @@
         send(fresh_all.at[s], fresh_all.at[s], s_fresh.at[k], r_fresh.at[k], {"seq": peers[k]})
         for k in range(1, n)
     ]
-    total, copies = along_z(1, part_q, xrecv_q, zsend_q, zrecv_q)
-    total = finish(total, copies, zrecv_q)
+    total = finish(q_own, q_copies, zrecv_q)
     heads = total.shape[1] // head
     for h in range(heads):
         q_rows[pl.ds(h * new_dev, new_dev), :] = turn(
@@ -441,7 +477,6 @@
     old = cache_all[...].reshape(kept, 2 * head)
     new = fresh_all[...].reshape(n * new_dev, 2 * head)
     queries = q_rows[...]
-    contract = (((1,), (1,)), ((), ()))
     scale = 1.0 / math.sqrt(head)
     old_score = (
         lax.dot_general(queries, old[:, :head], contract, preferred_element_type=jnp.float32) * scale
@@ -503,9 +538,13 @@
     chunks = width // 512
     vm, dma = pltpu.VMEM, pltpu.SemaphoreType.DMA
     scratch = [
+        vm((feat, toks), bf),
+        vm((1, toks), jnp.int32),
+        pltpu.SMEM((n,), jnp.int32),
+        vm((width // 128, 128), f32),
         vm((feat, width), bf),
-        vm((depth, qcols), bf),
-        vm((depth, kvcols), bf),
+        vm((XS, depth, qcols), bf),
+        vm((XS, depth, kvcols), bf),
         vm((new_dev, head), f32),
         vm((new_dev, head), f32),
         vm((n, cached, kvcols), bf),
@@ -514,21 +553,17 @@
         vm((chunks, new_dev, 512), f32),
         vm((chunks, half, 512), f32),
         vm((half, width), f32),
-        vm((n, half, depth), bf),
-        vm((n, 2, half, depth), bf),
-        vm((n, new_dev, kvcols), f32),
-        vm((n, new_dev, qcols), f32),
-        vm((zs, new_dev, kvcols), bf),
-        vm((zs, new_dev, kvcols), bf),
+        vm((zs, half, depth * XS), bf),
+        vm((zs, 2, half, depth * XS), bf),
+        vm((zs, new_dev, kvcols), f32),
+        vm((zs, new_dev, qcols), f32),
         vm((zs - 1, new_dev, kvcols), bf),
         vm((zs - 1, new_dev, kvcols), bf),
-        vm((zs, new_dev, qcols), bf),
-        vm((zs, new_dev, qcols), bf),
         vm((zs - 1, new_dev, qcols), bf),
         vm((zs - 1, new_dev, qcols), bf),
         vm((n, new_dev, kvcols), bf),
         vm((qcols // head * new_dev, head), bf),
-        dma((6,)),
+        dma((10,)),
         dma((n,)),
         dma((n,)),
         dma((n,)),
@@ -539,38 +574,34 @@
         dma((n,)),
         dma((n,)),
         dma((n,)),
+        dma((4,)),
+        dma((4,)),
+        dma((4,)),
+        dma((4,)),
         dma((2, zs)),
         dma((2, zs)),
-        dma((2, zs)),
-        dma((2, zs)),
         dma((n,)),
         dma((n,)),
     ]
     in_vmem = pl.BlockSpec(memory_space=pltpu.VMEM)
-    anywhere = pl.BlockSpec(memory_space=pl.ANY)
+    in_hbm = pl.BlockSpec(memory_space=pltpu.HBM)
     attended, fresh = pl.pallas_call(
         functools.partial(fused_kernel, n),
         out_shape=(
             jax.ShapeDtypeStruct((new_dev, qcols), bf),
             jax.ShapeDtypeStruct((new_dev, kvcols), bf),
         ),
-        in_specs=[
-            in_vmem,
-            in_vmem,
-            pl.BlockSpec(memory_space=pltpu.SMEM),
-            in_vmem,
-        ]
-        + [anywhere] * 6,
+        in_specs=[in_hbm] * 10,
         out_specs=(in_vmem, in_vmem),
         scratch_shapes=scratch,
         compiler_params=pltpu.CompilerParams(
-            collective_id=0, has_side_effects=True, vmem_limit_bytes=48 * 1024 * 1024
+            collective_id=0, has_side_effects=True, vmem_limit_bytes=60 * 1024 * 1024
         ),
     )(
-        vis_tokens,
+        vis_tokens.T,
         merge_target.reshape(1, toks),
         merged_counts,
-        norm_gain.reshape(1, width),
+        norm_gain.reshape(width // 128, 128),
         proj_weight,
         query_weight,
         keyval_weight.reshape(depth, kvcols),
@@ -595,7 +626,8 @@
         P("seq", "mdl", None),
         P(("grp", "seq"), "mdl", None),
     )
-    per_device = fused_plan if mesh.shape["seq"] == 8 else plain_plan
+    small = mesh.shape["seq"] == 8 and mesh.shape["grp"] == 2
+    per_device = fused_plan if small else plain_plan
     return jax.shard_map(
         per_device,
         mesh=mesh,

time: 62.3 us -> 55.8 us (0.90)
  local copies, waits for them, and re-layouts: 11.2 us -> 2.93 us
  Pallas kernels: 50 us -> 52.1 us
    unnamed x19 -> x2, local copies, waits for them, and re-layouts: 10.5 us -> 2.93 us
    pallas_call x1, Pallas kernels: 50 us -> 52.1 us  [fused_plan(): pl.pallas_call(functools.partial(fused_kernel, n), out_shape=(jax.ShapeDt...]
    reshape x1 -> x0, local copies, waits for them, and re-layouts: 0.73 us -> none  [fused_plan(): norm_gain.reshape(1, width)]
where the time goes in v2:
time: 55.8 us; the launch traced here: 55.6 us
  Pallas kernels  52.1 us (93%)
  local copies, waits for them, and re-layouts  2.93 us (5%)
  between operations  0.64 us (1%)
    pallas_call x1, Pallas kernels, fused_plan(): pl.pallas_call(functools.partial(fused_kernel, n), out_shape=(jax.ShapeDt...  52.1 us
    unnamed x2, local copies, waits for them, and re-layouts  2.93 us

profile of v2, /device:TPU:0, one launch (start us, length us, event | category | flops | bytes accessed | tf_op | source)
XLA Modules:
  0.0 55.6 jit_solution(8892310291898144250)
XLA Ops:
  0.6 52.1 %shard_map.113 = (bf16[64,896]{1,0:T(8,128)(2,1)}, bf16[64,256]{1,0:T(8,128)(2,1)}) custom-call(bf16[576,128]{1,0:T(8,128)(2,1)} %bitcast.8, s32[1,128]{1,0:T(1,128)} %bitcast.13, s32[8]{0:T(128)} %counts_hbm.1, f32[28,128]{1,0:T(8,128)} %bitcast.11, bf16[576,3584]{1,0:T(8,128)(2,1)} %proj_hbm.1, bf16[448,896]{1,0:T(8,128)(2,1)} %wq_hbm.1, ...), custom_call_target="tpu_custom_call" | custom-call | tf_op jit(solution)/shard_map/pallas_call | solution.py:588
  52.7 1.6 %copy.14 = bf16[64,1,896]{2,0,1:T(8,128)(2,1)} copy(bf16[64,1,896]{2,0,1:T(8,128)(2,1)} %bitcast.9) | data formatting | bytes 229376
  54.3 1.4 %copy.15 = bf16[64,1,1,256]{3,0,2,1:T(8,128)(2,1)} copy(bf16[64,1,1,256]{3,0,2,1:T(8,128)(2,1)} %bitcast.10) | data formatting | bytes 65536

commit v3 on v2

--- a/solution.py
+++ b/solution.py
@@ -174,6 +174,7 @@
 
 def fused_kernel(
     n,
+    w_rows,
     vis_hbm,
     target_hbm,
     counts_hbm,
@@ -309,12 +310,11 @@
         for k in range(1, n)
     ]
     depth = wq.shape[1]
-    part_rows = depth // 4
     loads[4].wait()
     loads[5].wait()
     pieces = []
-    for c in range(2):
-        at = pl.ds(pl.multiple_of((g * 2 + c) * part_rows, 16), part_rows)
+    for first, count in w_rows:
+        at = pl.ds(pl.multiple_of(g * (depth // 2) + first, 16), count)
         for which, weight in enumerate((wkv, wq)):
             pieces.append((weight.at[x, at], weight.at[1 - x, at]))
     straight = [
@@ -331,9 +331,24 @@
 
     loads[3].wait()
     cache_copies = [
-        send(cache_all.at[s], cache_all.at[s], s_cache.at[k], r_cache.at[k], {"seq": peers[k]})
-        for k in range(1, n)
+        send(
+            cache_all.at[s],
+            cache_all.at[s],
+            s_cache.at[k],
+            r_cache.at[k],
+            {"seq": (z + k) % zs * XS + x},
+        )
+        for k in range(1, zs)
     ]
+
+    def share_x(buffer, copies, ssem, rsem):
+        shared = [send(buffer.at[s], buffer.at[s], ssem.at[zs], rsem.at[zs], beside_x)]
+        for k in range(1, zs):
+            copies[k - 1].wait()
+            came = buffer.at[(z + zs - k) % zs * XS + x]
+            shared.append(send(came, came, ssem.at[zs + k], rsem.at[zs + k], beside_x))
+        return shared
+
     incoming[s] = packed[s]
 
     column = lax.broadcasted_iota(jnp.int32, (new_dev, slots), 1)
@@ -406,12 +421,13 @@
         )
     norm_all[z, m] = norm_send[z]
     forwards = [send(norm_all.at[z, m], norm_all.at[z, m], s_fwd.at[0], r_fwd.at[0], mate)]
-    crossing = pass_on((0, 1))
+    early = len(pieces) // 2
+    crossing = pass_on(range(early))
     for k in range(1, zs):
         norm_copies[k - 1].wait()
         came = norm_all.at[(z + zs - k) % zs, m]
         forwards.append(send(came, came, s_fwd.at[k], r_fwd.at[k], mate))
-    crossing = crossing + pass_on((2, 3))
+    crossing = crossing + pass_on(range(early, len(pieces)))
     for copy in forwards:
         copy.wait()
     for copy in crossing:
@@ -447,6 +463,7 @@
     head = cos_t.shape[1]
     kv_own, kv_copies = along_z(0, wkv, part_kv, zsend_kv, zrecv_kv)
     q_own, q_copies = along_z(1, wq, part_q, zsend_q, zrecv_q)
+    cache_shared = share_x(cache_all, cache_copies, s_cache, r_cache)
     loads[7].wait()
     loads[8].wait()
     cosine, sine = cos_t[...], sin_t[...]
@@ -459,18 +476,25 @@
     fresh_all[s] = fresh
     newkv_ref[...] = fresh
     fresh_copies = [
-        send(fresh_all.at[s], fresh_all.at[s], s_fresh.at[k], r_fresh.at[k], {"seq": peers[k]})
-        for k in range(1, n)
+        send(
+            fresh_all.at[s],
+            fresh_all.at[s],
+            s_fresh.at[k],
+            r_fresh.at[k],
+            {"seq": (z + k) % zs * XS + x},
+        )
+        for k in range(1, zs)
     ]
+    fresh_shared = share_x(fresh_all, fresh_copies, s_fresh, r_fresh)
     total = finish(q_own, q_copies, zrecv_q)
     heads = total.shape[1] // head
     for h in range(heads):
         q_rows[pl.ds(h * new_dev, new_dev), :] = turn(
             total[:, h * head : (h + 1) * head]
         ).astype(jnp.bfloat16)
-    for copy in cache_copies:
+    for copy in cache_shared:
         copy.wait()
-    for copy in fresh_copies:
+    for copy in fresh_shared:
         copy.wait()
 
     kept = cache_all.shape[0] * cache_all.shape[1]
@@ -536,6 +560,8 @@
     sin_table = np.concatenate([-np.sin(angles), np.sin(angles)], axis=-1).astype(np.float32)
     bf, f32 = jnp.bfloat16, jnp.float32
     chunks = width // 512
+    w_rows = [(at, min(64, depth // 2 - at)) for at in range(0, depth // 2, 64)]
+    pieces = 2 * len(w_rows)
     vm, dma = pltpu.VMEM, pltpu.SemaphoreType.DMA
     scratch = [
         vm((feat, toks), bf),
@@ -574,10 +600,10 @@
         dma((n,)),
         dma((n,)),
         dma((n,)),
-        dma((4,)),
-        dma((4,)),
-        dma((4,)),
-        dma((4,)),
+        dma((pieces,)),
+        dma((pieces,)),
+        dma((pieces,)),
+        dma((pieces,)),
         dma((2, zs)),
         dma((2, zs)),
         dma((n,)),
@@ -586,7 +612,7 @@
     in_vmem = pl.BlockSpec(memory_space=pltpu.VMEM)
     in_hbm = pl.BlockSpec(memory_space=pltpu.HBM)
     attended, fresh = pl.pallas_call(
-        functools.partial(fused_kernel, n),
+        functools.partial(fused_kernel, n, w_rows),
         out_shape=(
             jax.ShapeDtypeStruct((new_dev, qcols), bf),
             jax.ShapeDtypeStruct((new_dev, kvcols), bf),

time: 55.8 us -> 55.2 us (0.989)
  Pallas kernels: 52.1 us -> 51.4 us
    pallas_call x1, Pallas kernels: 52.1 us -> 51.4 us  [fused_plan(): pl.pallas_call(functools.partial(fused_kernel, n, w_rows), out_shape=(jax...]
where the time goes in v3:
time: 55.2 us; the launch traced here: 55 us
  Pallas kernels  51.4 us (93%)
  local copies, waits for them, and re-layouts  2.93 us (5%)
  between operations  0.64 us (1%)
    pallas_call x1, Pallas kernels, fused_plan(): pl.pallas_call(functools.partial(fused_kernel, n, w_rows), out_shape=(jax...  51.4 us
    unnamed x2, local copies, waits for them, and re-layouts  2.93 us

profile of v3, /device:TPU:0, one launch (start us, length us, event | category | flops | bytes accessed | tf_op | source)
XLA Modules:
  0.0 55.0 jit_solution(1995064290049783665)
XLA Ops:
  0.6 51.4 %shard_map.113 = (bf16[64,896]{1,0:T(8,128)(2,1)}, bf16[64,256]{1,0:T(8,128)(2,1)}) custom-call(bf16[576,128]{1,0:T(8,128)(2,1)} %bitcast.8, s32[1,128]{1,0:T(1,128)} %bitcast.13, s32[8]{0:T(128)} %counts_hbm.1, f32[28,128]{1,0:T(8,128)} %bitcast.11, bf16[576,3584]{1,0:T(8,128)(2,1)} %proj_hbm.1, bf16[448,896]{1,0:T(8,128)(2,1)} %wq_hbm.1, ...), custom_call_target="tpu_custom_call" | custom-call | tf_op jit(solution)/shard_map/pallas_call | solution.py:614
  52.1 1.6 %copy.14 = bf16[64,1,896]{2,0,1:T(8,128)(2,1)} copy(bf16[64,1,896]{2,0,1:T(8,128)(2,1)} %bitcast.9) | data formatting | bytes 229376
  53.6 1.4 %copy.15 = bf16[64,1,1,256]{3,0,2,1:T(8,128)(2,1)} copy(bf16[64,1,1,256]{3,0,2,1:T(8,128)(2,1)} %bitcast.10) | data formatting | bytes 65536

commit v4 on v3

--- a/solution.py
+++ b/solution.py
@@ -313,10 +313,9 @@
     loads[4].wait()
     loads[5].wait()
     pieces = []
-    for first, count in w_rows:
+    for weight, first, count in [(wkv, 0, depth // 2)] + [(wq, *rows) for rows in w_rows]:
         at = pl.ds(pl.multiple_of(g * (depth // 2) + first, 16), count)
-        for which, weight in enumerate((wkv, wq)):
-            pieces.append((weight.at[x, at], weight.at[1 - x, at]))
+        pieces.append((weight.at[x, at], weight.at[1 - x, at]))
     straight = [
         send(src, src, s_w.at[at], r_w.at[at], beside_x) for at, (src, _) in enumerate(pieces)
     ]
@@ -421,7 +420,7 @@
         )
     norm_all[z, m] = norm_send[z]
     forwards = [send(norm_all.at[z, m], norm_all.at[z, m], s_fwd.at[0], r_fwd.at[0], mate)]
-    early = len(pieces) // 2
+    early = 1 + len(pieces) // 2
     crossing = pass_on(range(early))
     for k in range(1, zs):
         norm_copies[k - 1].wait()
@@ -430,8 +429,7 @@
     crossing = crossing + pass_on(range(early, len(pieces)))
     for copy in forwards:
         copy.wait()
-    for copy in crossing:
-        copy.wait()
+    crossing[0].wait()
 
     lhs = norm_all[...].reshape(zs * new_dev, wide)
     order = [(z + k) % zs for k in range(1, zs)]
@@ -462,7 +460,6 @@
 
     head = cos_t.shape[1]
     kv_own, kv_copies = along_z(0, wkv, part_kv, zsend_kv, zrecv_kv)
-    q_own, q_copies = along_z(1, wq, part_q, zsend_q, zrecv_q)
     cache_shared = share_x(cache_all, cache_copies, s_cache, r_cache)
     loads[7].wait()
     loads[8].wait()
@@ -485,6 +482,9 @@
         )
         for k in range(1, zs)
     ]
+    for copy in crossing[1:]:
+        copy.wait()
+    q_own, q_copies = along_z(1, wq, part_q, zsend_q, zrecv_q)
     fresh_shared = share_x(fresh_all, fresh_copies, s_fresh, r_fresh)
     total = finish(q_own, q_copies, zrecv_q)
     heads = total.shape[1] // head
@@ -561,7 +561,7 @@
     bf, f32 = jnp.bfloat16, jnp.float32
     chunks = width // 512
     w_rows = [(at, min(64, depth // 2 - at)) for at in range(0, depth // 2, 64)]
-    pieces = 2 * len(w_rows)
+    pieces = 1 + len(w_rows)
     vm, dma = pltpu.VMEM, pltpu.SemaphoreType.DMA
     scratch = [
         vm((feat, toks), bf),
@@ -614,8 +614,8 @@
     attended, fresh = pl.pallas_call(
         functools.partial(fused_kernel, n, w_rows),
         out_shape=(
-            jax.ShapeDtypeStruct((new_dev, qcols), bf),
-            jax.ShapeDtypeStruct((new_dev, kvcols), bf),
+            pltpu.VMEM((new_dev, qcols), bf),
+            pltpu.VMEM((new_dev, kvcols), bf),
         ),
         in_specs=[in_hbm] * 10,
         out_specs=(in_vmem, in_vmem),

time: 55.2 us -> 44.6 us (0.81)
  Pallas kernels: 51.4 us -> 42.5 us
  local copies, waits for them, and re-layouts: 2.93 us -> 1.26 us
    pallas_call x1, Pallas kernels: 51.4 us -> 42.5 us  [fused_plan(): pl.pallas_call(functools.partial(fused_kernel, n, w_rows), out_shape=(plt...]
    unnamed x2, local copies, waits for them, and re-layouts: 2.93 us -> 1.26 us
where the time goes in v4:
time: 44.6 us; the launch traced here: 44.5 us
  Pallas kernels  42.5 us (95%)
  local copies, waits for them, and re-layouts  1.26 us (3%)
  between operations  0.64 us (1%)
    pallas_call x1, Pallas kernels, fused_plan(): pl.pallas_call(functools.partial(fused_kernel, n, w_rows), out_shape=(plt...  42.5 us
    unnamed x2, local copies, waits for them, and re-layouts  1.26 us

profile of v4, /device:TPU:0, one launch (start us, length us, event | category | flops | bytes accessed | tf_op | source)
XLA Modules:
  0.0 44.5 jit_solution(1739463337201437438)
XLA Ops:
  0.6 42.5 %shard_map.113 = (bf16[64,896]{1,0:T(8,128)(2,1)S(1)}, bf16[64,256]{1,0:T(8,128)(2,1)S(1)}) custom-call(bf16[576,128]{1,0:T(8,128)(2,1)} %bitcast.10, s32[1,128]{1,0:T(1,128)} %bitcast.13, s32[8]{0:T(128)} %counts_hbm.1, f32[28,128]{1,0:T(8,128)} %bitcast.11, bf16[576,3584]{1,0:T(8,128)(2,1)} %proj_hbm.1, bf16[448,896]{1,0:T(8,128)(2,1)} %wq_hbm.1, ...), custom_call_target="tpu_custom_call" | custom-call | tf_op jit(solution)/shard_map/pallas_call | solution.py:614
  43.2 0.6 %copy.14 = bf16[64,1,896]{2,0,1:T(8,128)(2,1)} copy(bf16[64,1,896]{2,0,1:T(8,128)(2,1)S(1)} %bitcast.7) | data formatting | bytes 229376
  43.8 0.6 %copy.15 = bf16[64,1,1,256]{3,0,2,1:T(8,128)(2,1)} copy(bf16[64,1,1,256]{3,0,2,1:T(8,128)(2,1)S(1)} %bitcast.8) | data formatting | bytes 65536

commit v5 on v4

--- a/solution.py
+++ b/solution.py
@@ -174,7 +174,7 @@
 
 def fused_kernel(
     n,
-    w_rows,
+    w_cols,
     vis_hbm,
     target_hbm,
     counts_hbm,
@@ -313,9 +313,10 @@
     loads[4].wait()
     loads[5].wait()
     pieces = []
-    for weight, first, count in [(wkv, 0, depth // 2)] + [(wq, *rows) for rows in w_rows]:
-        at = pl.ds(pl.multiple_of(g * (depth // 2) + first, 16), count)
-        pieces.append((weight.at[x, at], weight.at[1 - x, at]))
+    at = pl.ds(pl.multiple_of(g * (depth // 2), 16), depth // 2)
+    pieces.append((wkv.at[x, at], wkv.at[1 - x, at]))
+    for cols in w_cols:
+        pieces.append((wq.at[x, at, pl.ds(*cols)], wq.at[1 - x, at, pl.ds(*cols)]))
     straight = [
         send(src, src, s_w.at[at], r_w.at[at], beside_x) for at, (src, _) in enumerate(pieces)
     ]
@@ -482,11 +483,20 @@
         )
         for k in range(1, zs)
     ]
-    for copy in crossing[1:]:
-        copy.wait()
-    q_own, q_copies = along_z(1, wq, part_q, zsend_q, zrecv_q)
+    q_sums = []
+    for c, cols in enumerate(w_cols):
+        crossing[1 + c].wait()
+        q_sums.append(
+            along_z(1 + c, *(ref.at[:, :, pl.ds(*cols)] for ref in (wq, part_q, zsend_q, zrecv_q)))
+        )
     fresh_shared = share_x(fresh_all, fresh_copies, s_fresh, r_fresh)
-    total = finish(q_own, q_copies, zrecv_q)
+    total = jnp.concatenate(
+        [
+            finish(own, copies, zrecv_q.at[:, :, pl.ds(*cols)])
+            for (own, copies), cols in zip(q_sums, w_cols)
+        ],
+        axis=1,
+    )
     heads = total.shape[1] // head
     for h in range(heads):
         q_rows[pl.ds(h * new_dev, new_dev), :] = turn(
@@ -560,8 +570,8 @@
     sin_table = np.concatenate([-np.sin(angles), np.sin(angles)], axis=-1).astype(np.float32)
     bf, f32 = jnp.bfloat16, jnp.float32
     chunks = width // 512
-    w_rows = [(at, min(64, depth // 2 - at)) for at in range(0, depth // 2, 64)]
-    pieces = 1 + len(w_rows)
+    w_cols = [(at, min(256, qcols - at)) for at in range(0, qcols, 256)]
+    pieces = 1 + len(w_cols)
     vm, dma = pltpu.VMEM, pltpu.SemaphoreType.DMA
     scratch = [
         vm((feat, toks), bf),
@@ -604,15 +614,15 @@
         dma((pieces,)),
         dma((pieces,)),
         dma((pieces,)),
-        dma((2, zs)),
-        dma((2, zs)),
+        dma((pieces, zs)),
+        dma((pieces, zs)),
         dma((n,)),
         dma((n,)),
     ]
     in_vmem = pl.BlockSpec(memory_space=pltpu.VMEM)
     in_hbm = pl.BlockSpec(memory_space=pltpu.HBM)
     attended, fresh = pl.pallas_call(
-        functools.partial(fused_kernel, n, w_rows),
+        functools.partial(fused_kernel, n, w_cols),
         out_shape=(
             pltpu.VMEM((new_dev, qcols), bf),
             pltpu.VMEM((new_dev, kvcols), bf),

time: 44.6 us -> 46.2 us (1.036)
  Pallas kernels: 42.5 us -> 44.2 us
    pallas_call x1, Pallas kernels: 42.5 us -> 44.2 us  [fused_plan(): pl.pallas_call(functools.partial(fused_kernel, n, w_cols), out_shape=(plt...]
where the time goes in v5:
time: 46.2 us; the launch traced here: 46.1 us
  Pallas kernels  44.2 us (96%)
  local copies, waits for them, and re-layouts  1.26 us (3%)
  between operations  0.64 us (1%)
    pallas_call x1, Pallas kernels, fused_plan(): pl.pallas_call(functools.partial(fused_kernel, n, w_cols), out_shape=(plt...  44.2 us
    unnamed x2, local copies, waits for them, and re-layouts  1.26 us

profile of v5, /device:TPU:0, one launch (start us, length us, event | category | flops | bytes accessed | tf_op | source)
XLA Modules:
  0.0 46.1 jit_solution(14914786382493145174)
XLA Ops:
  0.6 44.2 %shard_map.113 = (bf16[64,896]{1,0:T(8,128)(2,1)S(1)}, bf16[64,256]{1,0:T(8,128)(2,1)S(1)}) custom-call(bf16[576,128]{1,0:T(8,128)(2,1)} %bitcast.10, s32[1,128]{1,0:T(1,128)} %bitcast.13, s32[8]{0:T(128)} %counts_hbm.1, f32[28,128]{1,0:T(8,128)} %bitcast.11, bf16[576,3584]{1,0:T(8,128)(2,1)} %proj_hbm.1, bf16[448,896]{1,0:T(8,128)(2,1)} %wq_hbm.1, ...), custom_call_target="tpu_custom_call" | custom-call | tf_op jit(solution)/shard_map/pallas_call | solution.py:624
  44.8 0.6 %copy.14 = bf16[64,1,896]{2,0,1:T(8,128)(2,1)} copy(bf16[64,1,896]{2,0,1:T(8,128)(2,1)S(1)} %bitcast.7) | data formatting | bytes 229376
  45.5 0.6 %copy.15 = bf16[64,1,1,256]{3,0,2,1:T(8,128)(2,1)} copy(bf16[64,1,1,256]{3,0,2,1:T(8,128)(2,1)S(1)} %bitcast.8) | data formatting | bytes 65536
